TPU v7x, 32 devices: a whole 2x2x4 slice. The times are simulated.
32 devices in a mesh: pole: 2 (over y), row: 16 (over z, x, core).
Axes of the slice: x: 2, y: 2, z: 4, core: 2. Of those that a mesh axis runs over, the one named last changes fastest.
Arguments:
- inverse_rows: bfloat16 [4096, 2048], P(('pole', 'row')), parts along dimension 0, may hold values from -6 to 6
- lower_panels: bfloat16 [2, 4096, 384], P(None, ('pole', 'row')), parts along dimension 1, may hold values from -0.1875 to 0.1875
- link_block: bfloat16 [768, 384], P('pole'), parts along dimension 0, may hold values from -0.3125 to 0.3125
- diag_inverse: float32 [2, 768, 384], P(None, 'pole'), parts along dimension 1, may hold values from -6 to 6
- pattern: int32 [2, 32], replicated, may hold values from 0 to 1, as said below
Outputs:
- panel_first: bfloat16 [4096, 384], P(('pole', 'row')), parts along dimension 0
- panel_second: bfloat16 [4096, 384], P(('pole', 'row')), parts along dimension 0
- diag_first: float32 [768, 384], P('pole'), parts along dimension 0
- cross: float32 [768, 384], P('pole'), parts along dimension 0
- diag_second: float32 [768, 384], P('pole'), parts along dimension 0
There are 2 independent parts, one for each index of `pole`. A program takes and returns all parts, laid end to end along the dimension named above; an argument that names none is the same for every part. Nothing has to cross between parts.
Inputs may be any that keep to these rules, and one draw needn't show every extreme that they name: `pattern`: each entry is 0 or 1. Among the 2 blocks of each aligned group (the blocks of one device), exactly 2 are marked in row 0 and exactly 1 in row 1; a block marked in row 1 is marked in row 0 too.
All inputs are finite; a program needn't handle non-finite values.
Results may differ from a plain program's by a relative error of at most 0.0043.
Values may be sent and summed in bfloat16 or wider, within the bound.
A program may use at most 128 MiB of HBM per device.

v0:
```python
import jax
import jax.numpy as jnp
from jax import lax
from jax.sharding import PartitionSpec as P

AW = 64
KEEP_UP = 2
KEEP_LOW = 1


def kept_table(marks, blocks_dev, amount):
    order = jnp.argsort(1 - marks, axis=1, stable=True)[:, :amount]
    groups = jnp.arange(marks.shape[0], dtype=jnp.int32)[:, None] * blocks_dev
    blocks = groups + order
    rows = blocks[:, :, None] * AW + jnp.arange(AW, dtype=jnp.int32)[None, None, :]
    return (order, rows.reshape(-1))


def pack_rows(masked, order_all, own_index, blocks_dev, width):
    own_order = lax.dynamic_index_in_dim(order_all, own_index, 0, keepdims=False)
    blocks = masked.reshape(blocks_dev, AW, width)
    return jnp.take(blocks, own_order, axis=0).reshape(-1, width)


def shards(inverse_rows, lower_panels, link_block, diag_inverse, pattern):
    rows_dev = inverse_rows.shape[0]
    blocks_dev = rows_dev // AW
    width = lower_panels.shape[2]
    own_index = lax.axis_index("row")
    first_block = own_index * blocks_dev
    own = lax.dynamic_slice_in_dim(pattern, first_block, blocks_dev, 1)
    own_keep = jnp.repeat(own, AW, axis=1)
    keep_low = own_keep.astype(jnp.bfloat16)
    keep_wide = own_keep.astype(jnp.float32)
    first_masked = lower_panels[0] * keep_low[0][:, None]
    second_masked = lower_panels[1] * keep_low[1][:, None]
    layout = pattern.reshape(2, -1, blocks_dev)
    order_up, table_up = kept_table(layout[0], blocks_dev, KEEP_UP)
    order_low, table_low = kept_table(layout[1], blocks_dev, KEEP_LOW)
    packed_up = pack_rows(first_masked, order_up, own_index, blocks_dev, width)
    packed_low = pack_rows(second_masked, order_low, own_index, blocks_dev, width)
    picked = table_up
    columns = jnp.take(inverse_rows, picked, axis=1)
    far_first = jnp.dot(
        columns,
        lax.all_gather(packed_up, "row", axis=0, tiled=True),
        preferred_element_type=jnp.float32,
    )
    panel_first = (-far_first * keep_wide[0][:, None]).astype(jnp.bfloat16)
    diag_partial = jnp.dot(first_masked.T, panel_first, preferred_element_type=jnp.float32)
    cross_partial = jnp.dot(panel_first.T, second_masked, preferred_element_type=jnp.float32)
    diag_total = lax.psum(diag_partial, "row")
    diag_first = diag_inverse[0] - diag_total
    picked = table_low
    columns = jnp.take(inverse_rows, picked, axis=1)
    far_second = jnp.dot(
        columns,
        lax.all_gather(packed_low, "row", axis=0, tiled=True),
        preferred_element_type=jnp.float32,
    )
    near = jnp.dot(panel_first, link_block, preferred_element_type=jnp.float32)
    panel_second = (-(far_second + near) * keep_wide[1][:, None]).astype(jnp.bfloat16)
    second_partial = jnp.dot(second_masked.T, panel_second, preferred_element_type=jnp.float32)
    cross_total, second_total = lax.psum((cross_partial, second_partial), "row")
    link_wide = link_block.astype(jnp.float32)
    cross = -(cross_total + jnp.dot(diag_first, link_wide, precision=lax.Precision.HIGHEST))
    diag_second = (
        diag_inverse[1]
        - second_total
        - jnp.dot(link_wide.T, cross, precision=lax.Precision.HIGHEST)
    )
    return (panel_first, panel_second, diag_first, cross, diag_second)


def solution(mesh):
    in_specs = (
        P(("pole", "row"), None),
        P(None, ("pole", "row"), None),
        P("pole", None),
        P(None, "pole", None),
        P(),
    )
    out_specs = (
        P(("pole", "row"), None),
        P(("pole", "row"), None),
        P("pole", None),
        P("pole", None),
        P("pole", None),
    )
    return jax.shard_map(shards, mesh=mesh, in_specs=in_specs, out_specs=out_specs, check_vma=False)
```

profile of v0, /device:TPU:0, one launch (start us, length us, event | category | flops | bytes accessed | tf_op | source)
XLA Modules:
  0.0 169.8 jit_solution(14011468482664586820)
XLA Ops:
  7.2 0.8 subtract_reduce_fusion
  8.2 0.6 sort.31
  8.8 0.2 dynamic-slice_reduce_fusion
  9.0 0.8 fusion.22
  9.8 0.1 broadcast_in_dim.64
  9.9 1.0 fusion.30
  11.0 0.6 gather_fusion.1
  11.6 0.7 bitcast_select_fusion
  12.6 0.1 add.167
  12.8 0.1 mul.100
  13.1 0.1 mul.106
  13.3 0.1 mul.103
  13.5 0.6 sort.32
  14.1 0.6 constant_dynamic-slice_fusion
  16.7 0.6 dynamic-slice.5
  17.4 0.1 broadcast_reduce_fusion
  17.8 0.3 copy.21
  18.1 3.2 %gather_fusion.2 = bf16[1024,128]{1,0:T(8,128)(2,1)S(1)} fusion(bf16[128,2048]{0,1:T(8,128)(2,1)S(1)} %copy.21, s32[1024]{0:T(1024)S(1)} %broadcast_clamp_fusion.1), kind=kCustom, calls=%fused_computation.2 | custom fusion | bytes 528384 | tf_op jit(solution)/shard_map/jit(_take)/gather | solution.py:55
  21.3 6.2 %gather_fusion = bf16[2048,128]{1,0:T(8,128)(2,1)S(1)} fusion(bf16[128,2048]{0,1:T(8,128)(2,1)S(1)} %copy.21, s32[2048]{0:T(1024)S(1)} %broadcast_clamp_fusion), kind=kCustom, calls=%fused_computation | custom fusion | bytes 1056768 | tf_op jit(solution)/shard_map/jit(_take)/gather | solution.py:43
  27.5 0.7 fusion.18
  28.2 25.5 %all-gather = bf16[1,1024,384]{2,1,0:T(8,128)(2,1)S(1)} all-gather(bf16[1,64,384]{2,1,0:T(8,128)(2,1)S(1)} %fusion.18), channel_id=2, replica_groups=mesh['pole'=2,'row'=16] {'row'}, dimensions={1}, use_global_device_ids=true | all-gather | bytes 835584 | tf_op jit(solution)/shard_map/all_gather | solution.py:58
  53.7 0.6 fusion.7
  54.3 2.3 %all-gather.3.cloned.1.call-done = bf16[2048,384]{1,0:T(8,128)(2,1)} async-done(((bf16[128,384]{1,0:T(8,128)(2,1)}), bf16[2048,384]{1,0:T(8,128)(2,1)}) %all-gather.3.cloned.1.call-update) | async-done | bytes 1572880 | tf_op jit(solution)/shard_map/all_gather | solution.py:46
  56.6 2.4 %fusion.5 = bf16[128,384]{1,0:T(8,128)(2,1)S(1)} fusion(bf16[2048,384]{1,0:T(8,128)(2,1)} %all-gather.3.cloned.1.call-done, bf16[2048,128]{1,0:T(8,128)(2,1)S(1)} %gather_fusion, pred[2048]{0:T(1024)(128)(4,1)S(1)} %compare_and_fusion, f32[128]{0:T(128)S(1)} %mul.92), kind=kOutput, calls=%fused_computation.12 | convolution fusion | flops 201736192 | bytes 2198016 | tf_op jit(solution)/shard_map/dot_general | solution.py:44
  59.0 1.1 fusion.15
  60.1 1.1 fusion.17
  61.2 0.2 fusion.6
  61.5 1.1 fusion.16
  62.7 96.8 %all-reduce.3.cloned.1.call-done = (f32[384,384]{1,0:T(8,128)}, f32[384,384]{1,0:T(8,128)}, f32[384,384]{1,0:T(8,128)}) async-done(((f32[384,384]{1,0:T(8,128)}, f32[384,384]{1,0:T(8,128)}, f32[384,384]{1,0:T(8,128)}), (f32[384,384]{1,0:T(8,128)}, f32[384,384]{1,0:T(8,128)}, f32[384,384]{1,0:T(8,128)})) %all-reduce.3.cloned.1.call-update) | async-done | bytes 1769488 | tf_op jit(solution)/shard_map/psum | solution.py:52
  159.5 1.2 bitcast_subtract_fusion.1
  160.7 0.7 fusion
  161.4 1.6 fusion.1
  (61 shorter events, 1.8 us)
Async XLA Ops:
  7.2 54.1 %copy-start = (bf16[384,384]{1,0:T(8,128)(2,1)S(1)}, bf16[384,384]{1,0:T(8,128)(2,1)}, u32[]{:S(2)}) copy-start(bf16[384,384]{1,0:T(8,128)(2,1)} %param.7) | copy-start | bytes 884740
  7.2 10.6 %copy-start.8 = (bf16[128,2048]{1,0:T(8,128)(2,1)S(1)}, bf16[128,2048]{1,0:T(8,128)(2,1)}, u32[]{:S(2)}) copy-start(bf16[128,2048]{1,0:T(8,128)(2,1)} %param.5) | copy-start | bytes 1572868
  7.2 49.4 %all-gather.3.cloned.1.call-start = ((), (), s32[]{:S(2)}) async-start(), calls=%async_computation | async-start | bytes 1671168 | tf_op jit(solution)/shard_map/all_gather | solution.py:46
  12.3 147.1 %all-reduce.3.cloned.1.call-start = ((), (), s32[]{:S(2)}) async-start(), calls=%async_computation.1 | async-start | bytes 3538944 | tf_op jit(solution)/shard_map/psum | solution.py:52
  53.7 5.2 %copy-start.4 = (bf16[2,128,384]{2,1,0:T(8,128)(2,1)S(1)}, bf16[2,128,384]{2,1,0:T(8,128)(2,1)}, u32[]{:S(2)}) copy-start(bf16[2,128,384]{2,1,0:T(8,128)(2,1)} %param.6) | copy-start | bytes 589828
  59.0 3.7 %copy-start.3 = (bf16[128,384]{1,0:T(8,128)(2,1)}, bf16[128,384]{1,0:T(8,128)(2,1)S(1)}, u32[]{:S(2)}) copy-start(bf16[128,384]{1,0:T(8,128)(2,1)S(1)} %fusion.5) | copy-start | bytes 294916
  61.2 98.2 %copy-start.5 = (f32[2,384,384]{2,1,0:T(8,128)S(1)}, f32[2,384,384]{2,1,0:T(8,128)}, u32[]{:S(2)}) copy-start(f32[2,384,384]{2,1,0:T(8,128)} %param.8) | copy-start | bytes 3538948
  61.5 99.2 %copy-start.9 = (bf16[128,384]{1,0:T(8,128)(2,1)}, bf16[128,384]{1,0:T(8,128)(2,1)S(1)}, u32[]{:S(2)}) copy-start(bf16[128,384]{1,0:T(8,128)(2,1)S(1)} %fusion.6) | copy-start | bytes 294916
  159.4 1.3 copy-start.7
  159.4 2.0 %copy-start.6 = (f32[384,384]{1,0:T(8,128)S(1)}, f32[384,384]{1,0:T(8,128)}, u32[]{:S(2)}) copy-start(f32[384,384]{1,0:T(8,128)} %get-tuple-element.24) | copy-start | bytes 1769476
  160.7 2.3 %copy-start.1 = (f32[384,384]{1,0:T(8,128)}, f32[384,384]{1,0:T(8,128)S(1)}, u32[]{:S(2)}) copy-start(f32[384,384]{1,0:T(8,128)S(1)} %bitcast_subtract_fusion.1) | copy-start | bytes 1769476
  161.4 1.6 copy-start.2
Sparse Core Ops, SparseCore 0:
  12.4 44.0 all-gather.2
  62.8 96.6 all-reduce.2
where the time goes:
time: 170 us
  waiting for transfers between devices  99.1 us (58%)
  blocking collectives  25.5 us (15%)
  between operations  16.2 us (10%)
  local copies, waits for them, and re-layouts  14.5 us (9%)
  matrix products  8.84 us (5%)
  other arithmetic  5.61 us (3%)
    psum x1, waiting for transfers between devices, shards(): diag_total = lax.psum(diag_partial, 'row')  96.8 us
    all_gather x1, blocking collectives, shards(): lax.all_gather(packed_low, 'row', axis=0, tiled=True)  25.5 us
    gather x2, local copies, waits for them, and re-layouts, shards(): columns = jnp.take(inverse_rows, picked, axis=1)  9.39 us
  transfers between devices with their start and end apart: 2, of which 2 were waited for; matrix products, arithmetic and copies ran while one was open for 8% of the time, Pallas kernels for 0%

commit v1 on v0

v1 whole, which is shorter than its diff:
```python
import functools

import jax
import jax.numpy as jnp
from jax import lax
from jax.experimental import pallas as pl
from jax.experimental.pallas import tpu as pltpu
from jax.sharding import PartitionSpec as P

AW = 64
MESH = pl.DeviceIdType.MESH
F32 = jnp.float32
BF16 = jnp.bfloat16


def dot(a, b):
    return jnp.dot(a, b, preferred_element_type=F32)


def dot_t(a, b):
    return lax.dot_general(a, b, (((0,), (0,)), ((), ())), preferred_element_type=F32)


def split2(x):
    hi = x.astype(BF16)
    lo = (x - hi.astype(F32)).astype(BF16)
    return hi, lo


def kernel(nz, pat, a_hbm, lp_hbm, l_hbm, d_hbm,
           p1_out, p2_out, d1_out, c_out, d2_out,
           a_v, g_v, h_v, su_v, sloc, l_v, d_v, p2_v,
           acc1, acc2, accd, accc, accs,
           in_sem, out_sem, z_send, x_send, c_send, recv):
    me = lax.axis_index("row")
    z = lax.div(me, 4)
    x = lax.rem(lax.div(me, 2), 2)
    c = lax.rem(me, 2)
    ox, oc = 1 - x, 1 - c

    def idx(zz, xx, cc):
        return (zz * 2 + xx) * 2 + cc

    cp_f = pltpu.make_async_copy(lp_hbm.at[0], g_v.at[me, pl.ds(0, 2 * AW)], in_sem.at[0])
    cp_s = pltpu.make_async_copy(lp_hbm.at[1], sloc, in_sem.at[1])
    cp_a = pltpu.make_async_copy(a_hbm, a_v, in_sem.at[2])
    cp_l = pltpu.make_async_copy(l_hbm, l_v, in_sem.at[3])
    cp_d = pltpu.make_async_copy(d_hbm, d_v, in_sem.at[4])
    for cp in (cp_f, cp_s, cp_a, cp_l, cp_d):
        cp.start()

    barrier = pltpu.get_barrier_semaphore()
    for target in (idx(z, ox, c), idx(z, x, oc)):
        pl.semaphore_signal(barrier, inc=1, device_id={"row": target}, device_id_type=MESH)

    @pl.when(z > 0)
    def _():
        pl.semaphore_signal(barrier, inc=1, device_id={"row": idx(z - 1, x, c)}, device_id_type=MESH)

    @pl.when(z < nz - 1)
    def _():
        pl.semaphore_signal(barrier, inc=1, device_id={"row": idx(z + 1, x, c)}, device_id_type=MESH)

    acc1[...] = jnp.zeros_like(acc1)
    acc2[...] = jnp.zeros_like(acc2)
    accd[...] = jnp.zeros_like(accd)
    accc[...] = jnp.zeros_like(accc)
    accs[...] = jnp.zeros_like(accs)

    low0 = pat[1, 2 * me]
    low1 = pat[1, 2 * me + 1]
    up0 = pat[0, 2 * me]
    up1 = pat[0, 2 * me + 1]

    def keep(mark, value):
        return jnp.where(mark != 0, value, jnp.zeros_like(value))

    cp_f.wait()
    for i, mark in enumerate((up0, up1)):
        rows = pl.ds(i * AW, AW)
        g_v[me, rows, :] = keep(mark, g_v[me, rows, :])
    cp_s.wait()
    g_v[me, pl.ds(2 * AW, AW), :] = jnp.where(low0 != 0, sloc[pl.ds(0, AW), :], sloc[pl.ds(AW, AW), :])

    pl.semaphore_wait(barrier, 2 + (z > 0).astype(jnp.int32) + (z < nz - 1).astype(jnp.int32))

    def remote(ph, buf, slot, send_sem, target):
        return pltpu.make_async_remote_copy(
            src_ref=buf.at[slot], dst_ref=buf.at[slot],
            send_sem=send_sem, recv_sem=recv.at[ph, slot],
            device_id={"row": target}, device_id_type=MESH)

    def zcopy(ph, buf, zz, way):
        return remote(ph, buf, idx(zz, x, c), z_send.at[ph, (way + 1) // 2, zz], idx(z + way, x, c))

    def xcopy(ph, buf, zz):
        return remote(ph, buf, idx(zz, x, c), x_send.at[ph, zz], idx(z, ox, c))

    def ccopy(ph, buf, zz, xx):
        return remote(ph, buf, idx(zz, xx, c), c_send.at[ph, zz * 2 + xx], idx(z, x, oc))

    def arrived(ph, buf, slot):
        remote(ph, buf, slot, c_send.at[ph, 0], idx(z, x, oc)).wait_recv()

    def inside(v):
        return jnp.logical_and(v >= 0, v < nz)

    def gather(ph, buf, pair):
        for way in (-1, 1):
            @pl.when(inside(z + way))
            def _():
                zcopy(ph, buf, z, way).start()
        xcopy(ph, buf, z).start()
        ccopy(ph, buf, z, x).start()

        def zstage(d, way):
            zz = z + way * d

            @pl.when(inside(zz))
            def _():
                arrived(ph, buf, idx(zz, x, c))

                @pl.when(inside(z - way))
                def _():
                    zcopy(ph, buf, zz, -way).start()
                xcopy(ph, buf, zz).start()
                ccopy(ph, buf, zz, x).start()

        def xstage(zz):
            arrived(ph, buf, idx(zz, ox, c))
            ccopy(ph, buf, zz, ox).start()

        def cstage(zz):
            arrived(ph, buf, idx(zz, x, oc))
            pair(zz * 2 + x)
            arrived(ph, buf, idx(zz, ox, oc))
            pair(zz * 2 + ox)

        zstage(1, -1)
        zstage(1, 1)
        xstage(z)
        cstage(z)

        def step(d, carry):
            zstage(d, -1)
            zstage(d, 1)
            for way in (-1, 1):
                zz = z + way * (d - 1)

                @pl.when(inside(zz))
                def _():
                    xstage(zz)
            for way in (-1, 1):
                zz = z + way * (d - 1)

                @pl.when(inside(zz))
                def _():
                    cstage(zz)
            return carry

        lax.fori_loop(2, nz + 1, step, 0)

    def drain(ph, buf):
        def step(zz, carry):
            for way in (-1, 1):
                sends = zz <= z if way == 1 else zz >= z

                @pl.when(jnp.logical_and(sends, inside(z + way)))
                def _():
                    zcopy(ph, buf, zz, way).wait_send()
            xcopy(ph, buf, zz).wait_send()
            ccopy(ph, buf, zz, 0).wait_send()
            ccopy(ph, buf, zz, 1).wait_send()
            return carry

        lax.fori_loop(0, nz, step, 0)

    cp_a.wait()
    cp_l.wait()
    cp_d.wait()

    width = l_v.shape[1]

    def f_pair(buf, p):
        return buf[pl.ds(2 * p, 2), pl.ds(0, 2 * AW), :].reshape(4 * AW, width)

    def s_pair(buf, p):
        return buf[pl.ds(2 * p, 2), pl.ds(2 * AW, AW), :].reshape(2 * AW, width)

    def pair_a(p):
        start = pl.multiple_of(p * 4 * AW, 4 * AW)
        a = a_v[:, pl.ds(start, 4 * AW)]
        acc1[...] += dot(a, f_pair(g_v, p))
        for i in range(4):
            su_v[pl.ds(pl.multiple_of(start + i * AW, AW), AW), :] = keep(
                pat[1, 4 * p + i], g_v[2 * p + i // 2, pl.ds(2 * AW, AW), :])
        acc2[...] += dot(a, su_v[pl.ds(start, 4 * AW), :])

    gather(0, g_v, pair_a)

    for i, mark in enumerate((up0, up1)):
        rows = pl.ds(i * AW, AW)
        h_v[me, rows, :] = keep(mark, (-acc1[rows, :])).astype(BF16)
    p1 = h_v[me, pl.ds(0, 2 * AW), :]
    far = -(acc2[...] + dot(p1, l_v[...]))
    far = far.astype(BF16)
    p2_v[pl.ds(0, AW), :] = keep(low0, far[:AW])
    p2_v[pl.ds(AW, AW), :] = keep(low1, far[AW:])
    h_v[me, pl.ds(2 * AW, AW), :] = jnp.where(low0 != 0, far[:AW], far[AW:])

    out1 = pltpu.make_async_copy(h_v.at[me, pl.ds(0, 2 * AW)], p1_out, out_sem.at[0])
    out2 = pltpu.make_async_copy(p2_v, p2_out, out_sem.at[1])
    out1.start()
    out2.start()

    def pair_b(p):
        start = pl.multiple_of(p * 4 * AW, 4 * AW)
        p1 = f_pair(h_v, p)
        accd[...] += dot_t(f_pair(g_v, p), p1)
        accc[...] += dot_t(p1, su_v[pl.ds(start, 4 * AW), :])
        accs[...] += dot_t(s_pair(g_v, p), s_pair(h_v, p))

    gather(1, h_v, pair_b)

    link = l_v[...]
    accd[...] = d_v[0] - accd[...]
    out3 = pltpu.make_async_copy(accd, d1_out, out_sem.at[2])
    out3.start()
    hi, lo = split2(accd[...])
    accc[...] = -(accc[...] + (dot(hi, link) + dot(lo, link)))
    out4 = pltpu.make_async_copy(accc, c_out, out_sem.at[3])
    out4.start()
    hi, lo = split2(accc[...])
    accs[...] = d_v[1] - accs[...] - (dot_t(link, hi) + dot_t(link, lo))
    out5 = pltpu.make_async_copy(accs, d2_out, out_sem.at[4])
    out5.start()
    drain(0, g_v)
    drain(1, h_v)
    for cp in (out1, out2, out3, out4, out5):
        cp.wait()


def shards(n, inverse_rows, lower_panels, link_block, diag_inverse, pattern):
    rows, total = inverse_rows.shape
    width = lower_panels.shape[2]
    nz = n // 4
    any_spec = pl.BlockSpec(memory_space=pl.ANY)
    out = jax.ShapeDtypeStruct
    return pl.pallas_call(
        functools.partial(kernel, nz),
        out_shape=(
            out((rows, width), BF16), out((rows, width), BF16),
            out((width, width), F32), out((width, width), F32), out((width, width), F32)),
        in_specs=[pl.BlockSpec(memory_space=pltpu.SMEM)] + [any_spec] * 4,
        out_specs=(any_spec,) * 5,
        scratch_shapes=[
            pltpu.VMEM((rows, total), BF16),
            pltpu.VMEM((n, 3 * AW, width), BF16),
            pltpu.VMEM((n, 3 * AW, width), BF16),
            pltpu.VMEM((total, width), BF16),
            pltpu.VMEM((rows, width), BF16),
            pltpu.VMEM((width, width), BF16),
            pltpu.VMEM((2, width, width), F32),
            pltpu.VMEM((rows, width), BF16),
            pltpu.VMEM((rows, width), F32),
            pltpu.VMEM((rows, width), F32),
            pltpu.VMEM((width, width), F32),
            pltpu.VMEM((width, width), F32),
            pltpu.VMEM((width, width), F32),
            pltpu.SemaphoreType.DMA((5,)),
            pltpu.SemaphoreType.DMA((5,)),
            pltpu.SemaphoreType.DMA((2, 2, nz)),
            pltpu.SemaphoreType.DMA((2, nz)),
            pltpu.SemaphoreType.DMA((2, 2 * nz)),
            pltpu.SemaphoreType.DMA((2, n)),
        ],
        compiler_params=pltpu.CompilerParams(
            collective_id=0, has_side_effects=True,
            vmem_limit_bytes=(62 if n > 32 else 32) * 2 ** 20),
    )(pattern, inverse_rows, lower_panels, link_block, diag_inverse)


def solution(mesh):
    in_specs = (
        P(("pole", "row"), None),
        P(None, ("pole", "row"), None),
        P("pole", None),
        P(None, "pole", None),
        P(),
    )
    out_specs = (
        P(("pole", "row"), None),
        P(("pole", "row"), None),
        P("pole", None),
        P("pole", None),
        P("pole", None),
    )
    return jax.shard_map(
        functools.partial(shards, mesh.shape["row"]), mesh=mesh,
        in_specs=in_specs, out_specs=out_specs, check_vma=False)
```

time: 170 us -> 55.7 us (0.33)
  waiting for transfers between devices: 99.1 us -> 0 us
  Pallas kernels: 0 us -> 45.7 us
  blocking collectives: 25.5 us -> 0 us
  between operations: 16.2 us -> 0.66 us
  matrix products: 8.84 us -> 0 us
  local copies, waits for them, and re-layouts: 14.5 us -> 8.6 us
  other arithmetic: 5.61 us -> 0 us
    psum x1 -> x0, waiting for transfers between devices: 96.8 us -> none  [shards(): diag_total = lax.psum(diag_partial, 'row')]
    pallas_call x0 -> x1, Pallas kernels: none -> 45.7 us  [shards(): pl.pallas_call(functools.partial(kernel, nz), out_shape=(out((rows, width...]
    all_gather x1 -> x0, blocking collectives: 25.5 us -> none  [shards(): lax.all_gather(packed_low, 'row', axis=0, tiled=True)]
    gather x4 -> x0, local copies, waits for them, and re-layouts: 10.5 us -> none  [the longest x2 9.39 us: shards(): columns = jnp.take(inverse_rows, picked, axis=1)]
    dot_general x8 -> x0, matrix products: 8.84 us -> none  [the longest x1 2.37 us: shards(): jnp.dot(columns, lax.all_gather(packed_up, 'row', axis=0, tiled=True), pr...]
    unnamed x21 -> x15, local copies, waits for them, and re-layouts: 0.33 us -> 8.6 us
    all_gather x1 -> x0, waiting for transfers between devices: 2.26 us -> none  [shards(): lax.all_gather(packed_up, 'row', axis=0, tiled=True)]
    sub x2 -> x0, other arithmetic: 2.01 us -> none  [the longest x1 1.22 us: shards(): diag_first = diag_inverse[0] - diag_total]
  transfers between devices with their start and end apart: 2 -> 0, of which waited for: 2 -> 0; matrix products, arithmetic and copies ran while one was open for 8% -> 0% of each run, Pallas kernels for 0% -> 0%
where the time goes in v1:
time: 55.7 us; the launch traced here: 54.9 us
  Pallas kernels  45.7 us (82%)
  local copies, waits for them, and re-layouts  8.6 us (15%)
  between operations  0.66 us (1%)
    pallas_call x1, Pallas kernels, shards(): pl.pallas_call(functools.partial(kernel, nz), out_shape=(out((rows, width...  45.7 us
    unnamed x15, local copies, waits for them, and re-layouts  8.6 us

profile of v1, /device:TPU:0, one launch (start us, length us, event | category | flops | bytes accessed | tf_op | source)
XLA Modules:
  0.0 54.9 jit_solution(4116183883135520308)
XLA Ops:
  0.6 0.0 copy-start
  0.6 1.3 %copy-done = f32[2,384,384]{2,1,0:T(8,128)S(1)} copy-done((f32[2,384,384]{2,1,0:T(8,128)S(1)}, f32[2,384,384]{2,1,0:T(8,128)}, u32[]{:S(2)}) %copy-start) | copy-done | bytes 1179672
  1.9 0.0 copy-start.1
  1.9 1.0 %copy-done.1 = bf16[128,2048]{1,0:T(8,128)(2,1)S(1)} copy-done((bf16[128,2048]{1,0:T(8,128)(2,1)S(1)}, bf16[128,2048]{1,0:T(8,128)(2,1)}, u32[]{:S(2)}) %copy-start.1) | copy-done | bytes 524312
  2.9 0.0 copy-start.2
  2.9 1.0 %copy-done.2 = bf16[384,384]{1,0:T(8,128)(2,1)S(1)} copy-done((bf16[384,384]{1,0:T(8,128)(2,1)S(1)}, bf16[384,384]{1,0:T(8,128)(2,1)}, u32[]{:S(2)}) %copy-start.2) | copy-done | bytes 294936
  3.9 0.0 copy-start.3
  3.9 0.9 %copy-done.3 = bf16[2,128,384]{2,1,0:T(8,128)(2,1)S(1)} copy-done((bf16[2,128,384]{2,1,0:T(8,128)(2,1)S(1)}, bf16[2,128,384]{2,1,0:T(8,128)(2,1)}, u32[]{:S(2)}) %copy-start.3) | copy-done | bytes 196632
  4.8 0.0 copy-start.4
  4.8 0.7 %copy-done.4 = s32[2,32]{1,0:T(2,128)S(1)} copy-done((s32[2,32]{1,0:T(2,128)S(1)}, s32[2,32]{1,0:T(2,128)}, u32[]{:S(2)}) %copy-start.4) | copy-done | bytes 280
  5.5 45.7 %shard_map.92 = (bf16[128,384]{1,0:T(8,128)(2,1)S(1)}, bf16[128,384]{1,0:T(8,128)(2,1)S(1)}, f32[384,384]{1,0:T(8,128)S(1)}, f32[384,384]{1,0:T(8,128)S(1)}, f32[384,384]{1,0:T(8,128)S(1)}) custom-call(s32[2,32]{1,0:T(2,128)S(1)} %copy-done.4, bf16[128,2048]{1,0:T(8,128)(2,1)S(1)} %copy-done.1, bf16[2,128,384]{2,1,0:T(8,128)(2,1)S(1)} %copy-done.3, ...), custom_call_target="tpu_custom_call" | custom-call | tf_op jit(solution)/shard_map/pallas_call | solution.py:249
  51.2 0.6 %copy.15 = bf16[128,384]{1,0:T(8,128)(2,1)} copy(bf16[128,384]{1,0:T(8,128)(2,1)S(1)} %get-tuple-element.10) | data formatting | bytes 196608
  51.8 0.6 %copy.16 = bf16[128,384]{1,0:T(8,128)(2,1)} copy(bf16[128,384]{1,0:T(8,128)(2,1)S(1)} %get-tuple-element.11) | data formatting | bytes 196608
  52.5 0.8 %copy.17 = f32[384,384]{1,0:T(8,128)} copy(f32[384,384]{1,0:T(8,128)S(1)} %get-tuple-element.12) | data formatting | bytes 1179648
  53.3 0.8 %copy.18 = f32[384,384]{1,0:T(8,128)} copy(f32[384,384]{1,0:T(8,128)S(1)} %get-tuple-element.13) | data formatting | bytes 1179648
  54.1 0.8 %copy.19 = f32[384,384]{1,0:T(8,128)} copy(f32[384,384]{1,0:T(8,128)S(1)} %get-tuple-element.14) | data formatting | bytes 1179648
Async XLA Ops:
  0.6 1.3 %copy-start = (f32[2,384,384]{2,1,0:T(8,128)S(1)}, f32[2,384,384]{2,1,0:T(8,128)}, u32[]{:S(2)}) copy-start(f32[2,384,384]{2,1,0:T(8,128)} %d_hbm.1) | copy-start | bytes 3538948
  1.9 1.0 %copy-start.1 = (bf16[128,2048]{1,0:T(8,128)(2,1)S(1)}, bf16[128,2048]{1,0:T(8,128)(2,1)}, u32[]{:S(2)}) copy-start(bf16[128,2048]{1,0:T(8,128)(2,1)} %a_hbm.1) | copy-start | bytes 1572868
  2.9 1.0 %copy-start.2 = (bf16[384,384]{1,0:T(8,128)(2,1)S(1)}, bf16[384,384]{1,0:T(8,128)(2,1)}, u32[]{:S(2)}) copy-start(bf16[384,384]{1,0:T(8,128)(2,1)} %l_hbm.1) | copy-start | bytes 884740
  3.9 0.9 %copy-start.3 = (bf16[2,128,384]{2,1,0:T(8,128)(2,1)S(1)}, bf16[2,128,384]{2,1,0:T(8,128)(2,1)}, u32[]{:S(2)}) copy-start(bf16[2,128,384]{2,1,0:T(8,128)(2,1)} %lp_hbm.1) | copy-start | bytes 589828
  4.8 0.7 %copy-start.4 = (s32[2,32]{1,0:T(2,128)S(1)}, s32[2,32]{1,0:T(2,128)}, u32[]{:S(2)}) copy-start(s32[2,32]{1,0:T(2,128)} %pat.1) | copy-start | bytes 772

commit v2 on v0

v2 whole, which is shorter than its diff:
```python
import functools

import jax
import jax.numpy as jnp
from jax import lax
from jax.experimental import pallas as pl
from jax.experimental.pallas import tpu as pltpu
from jax.sharding import PartitionSpec as P

AW = 64
MESH = pl.DeviceIdType.MESH
F32 = jnp.float32
BF16 = jnp.bfloat16


def dot(a, b):
    return jnp.dot(a, b, preferred_element_type=F32)


def dot_t(a, b):
    return lax.dot_general(a, b, (((0,), (0,)), ((), ())), preferred_element_type=F32)


def split2(x):
    hi = x.astype(BF16)
    lo = (x - hi.astype(F32)).astype(BF16)
    return hi, lo


def kernel(nz, pat, a_hbm, lp_hbm, l_hbm, d_hbm,
           p1_out, p2_out, d1_out, c_out, d2_out,
           a_v, f_v, s_v, p_v, q_v, su_v, sloc, l_v, d_v,
           acc1, acc2, accd, accc, accs,
           in_sem, z_send, x_send, c_send, recv):
    me = lax.axis_index("row")
    z = lax.div(me, 4)
    x = lax.rem(lax.div(me, 2), 2)
    c = lax.rem(me, 2)
    ox, oc = 1 - x, 1 - c
    width = l_v.shape[1]
    bufs = (f_v, s_v, p_v, q_v)
    upper, lower, first, second = range(4)

    def idx(zz, xx, cc):
        return (zz * 2 + xx) * 2 + cc

    cp_f = pltpu.make_async_copy(lp_hbm.at[0], f_v.at[me], in_sem.at[0])
    cp_s = pltpu.make_async_copy(lp_hbm.at[1], sloc, in_sem.at[1])
    cp_a = pltpu.make_async_copy(a_hbm, a_v, in_sem.at[2])
    cp_l = pltpu.make_async_copy(l_hbm, l_v, in_sem.at[3])
    cp_d = pltpu.make_async_copy(d_hbm, d_v, in_sem.at[4])
    for cp in (cp_f, cp_s, cp_a, cp_l, cp_d):
        cp.start()

    def inside(v):
        return jnp.logical_and(v >= 0, v < nz)

    barrier = pltpu.get_barrier_semaphore()
    for target in (idx(z, ox, c), idx(z, x, oc)):
        pl.semaphore_signal(barrier, inc=1, device_id={"row": target}, device_id_type=MESH)
    for way in (-1, 1):
        @pl.when(inside(z + way))
        def _():
            pl.semaphore_signal(barrier, inc=1, device_id={"row": idx(z + way, x, c)}, device_id_type=MESH)

    low0, low1 = pat[1, 2 * me], pat[1, 2 * me + 1]
    up0, up1 = pat[0, 2 * me], pat[0, 2 * me + 1]

    def keep(mark, value):
        return jnp.where(mark != 0, value, jnp.zeros_like(value))

    cp_f.wait()
    for i, mark in enumerate((up0, up1)):
        rows = pl.ds(i * AW, AW)
        f_v[me, rows, :] = keep(mark, f_v[me, rows, :])
    cp_s.wait()
    s_v[me] = jnp.where(low0 != 0, sloc[pl.ds(0, AW), :], sloc[pl.ds(AW, AW), :])

    pl.semaphore_wait(barrier, 2 + (z > 0).astype(jnp.int32) + (z < nz - 1).astype(jnp.int32))

    def remote(st, slot, send_sem, target):
        return pltpu.make_async_remote_copy(
            src_ref=bufs[st].at[slot], dst_ref=bufs[st].at[slot],
            send_sem=send_sem, recv_sem=recv.at[st, slot],
            device_id={"row": target}, device_id_type=MESH)

    def zcopy(st, zz, way):
        return remote(st, idx(zz, x, c), z_send.at[st, (way + 1) // 2, zz], idx(z + way, x, c))

    def xcopy(st, zz):
        return remote(st, idx(zz, x, c), x_send.at[st, zz], idx(z, ox, c))

    def ccopy(st, zz, xx):
        return remote(st, idx(zz, xx, c), c_send.at[st, zz * 2 + xx], idx(z, x, oc))

    def arrived(st, slot):
        remote(st, slot, c_send.at[st, 0], idx(z, x, oc)).wait_recv()

    def send_own(st):
        for way in (-1, 1):
            @pl.when(inside(z + way))
            def _():
                zcopy(st, z, way).start()
        xcopy(st, z).start()
        ccopy(st, z, x).start()

    def at_distance(d, do):
        for way in (-1, 1):
            @pl.when(inside(z + way * d))
            def _():
                do(z + way * d, way)

    def relay(st, zz, way):
        arrived(st, idx(zz, x, c))

        @pl.when(inside(z - way))
        def _():
            zcopy(st, zz, -way).start()

    def across(st, zz):
        xcopy(st, zz).start()
        ccopy(st, zz, x).start()

    def from_x(st, zz):
        arrived(st, idx(zz, ox, c))
        ccopy(st, zz, ox).start()

    def from_core(st, zz, pair):
        arrived(st, idx(zz, x, oc))
        pair(zz * 2 + x)
        arrived(st, idx(zz, ox, oc))
        pair(zz * 2 + ox)

    def gather(one, two, pair_one):
        def z_one(zz, way):
            relay(one, zz, way)
            across(one, zz)

        def z_two(zz, way):
            relay(two, zz, way)

        at_distance(1, z_one)
        at_distance(1, z_two)
        from_x(one, z)
        from_core(one, z, pair_one)

        def step(d, carry):
            at_distance(d, z_one)
            at_distance(d - 1, lambda zz, way: across(two, zz))
            at_distance(d, z_two)
            at_distance(d - 1, lambda zz, way: from_x(one, zz))
            at_distance(d - 1, lambda zz, way: from_core(one, zz, pair_one))
            return carry

        lax.fori_loop(2, nz + 1, step, 0)

    def finish(two, pair_two):
        from_x(two, z)

        def turn(d, carry):
            at_distance(d, lambda zz, way: from_x(two, zz))
            return carry

        lax.fori_loop(1, nz, turn, 0)
        from_core(two, z, pair_two)

        def turn_core(d, carry):
            at_distance(d, lambda zz, way: from_core(two, zz, pair_two))
            return carry

        lax.fori_loop(1, nz, turn_core, 0)

    def columns(p):
        return pl.multiple_of(p * 4 * AW, 4 * AW)

    def pair_of(buf, p):
        return buf[pl.ds(2 * p, 2)].reshape(2 * buf.shape[1], width)

    def pair_upper(p):
        acc1[...] += dot(a_v[:, pl.ds(columns(p), 4 * AW)], pair_of(f_v, p))

    def pair_lower(p):
        start = columns(p)
        for i in range(4):
            su_v[pl.ds(pl.multiple_of(start + i * AW, AW), AW), :] = keep(
                pat[1, 4 * p + i], s_v[2 * p + i // 2])
        acc2[...] += dot(a_v[:, pl.ds(start, 4 * AW)], su_v[pl.ds(start, 4 * AW), :])

    def pair_first(p):
        p1 = pair_of(p_v, p)
        accd[...] += dot_t(pair_of(f_v, p), p1)
        accc[...] += dot_t(p1, su_v[pl.ds(columns(p), 4 * AW), :])

    def pair_second(p):
        accs[...] += dot_t(pair_of(s_v, p), pair_of(q_v, p))

    send_own(upper)
    send_own(lower)
    for acc in (acc1, acc2, accd, accc, accs):
        acc[...] = jnp.zeros_like(acc)
    cp_a.wait()
    cp_l.wait()
    cp_d.wait()

    gather(upper, lower, pair_upper)
    for i, mark in enumerate((up0, up1)):
        rows = pl.ds(i * AW, AW)
        p_v[me, rows, :] = keep(mark, -acc1[rows, :]).astype(BF16)
    send_own(first)

    p1 = p_v[me]
    p1_out[...] = p1
    acc2[...] += dot(p1, l_v[...])
    finish(lower, pair_lower)
    far = (-acc2[...]).astype(BF16)
    q_v[me] = jnp.where(low0 != 0, far[:AW], far[AW:])
    send_own(second)
    p2_out[pl.ds(0, AW), :] = keep(low0, far[:AW])
    p2_out[pl.ds(AW, AW), :] = keep(low1, far[AW:])

    gather(first, second, pair_first)
    link = l_v[...]
    diag = d_v[0] - accd[...]
    d1_out[...] = diag
    hi, lo = split2(diag)
    cross = -(accc[...] + (dot(hi, link) + dot(lo, link)))
    c_out[...] = cross
    hi, lo = split2(cross)
    accs[...] = (dot_t(link, hi) + dot_t(link, lo)) - d_v[1]
    finish(second, pair_second)
    d2_out[...] = -accs[...]

    def drain(zz, carry):
        for st in range(4):
            for way in (-1, 1):
                sends = zz <= z if way == 1 else zz >= z

                @pl.when(jnp.logical_and(sends, inside(z + way)))
                def _():
                    zcopy(st, zz, way).wait_send()
            xcopy(st, zz).wait_send()
            ccopy(st, zz, 0).wait_send()
            ccopy(st, zz, 1).wait_send()
        return carry

    lax.fori_loop(0, nz, drain, 0)


def write_out(*refs):
    for source, target in zip(refs[:5], refs[5:]):
        target[...] = source[...]


def shards(n, inverse_rows, lower_panels, link_block, diag_inverse, pattern):
    rows, total = inverse_rows.shape
    width = lower_panels.shape[2]
    nz = n // 4
    any_spec = pl.BlockSpec(memory_space=pl.ANY)
    out = jax.ShapeDtypeStruct
    shapes = (
            out((rows, width), BF16), out((rows, width), BF16),
            out((width, width), F32), out((width, width), F32), out((width, width), F32))
    made = pl.pallas_call(
        functools.partial(kernel, nz),
        out_shape=shapes,
        in_specs=[pl.BlockSpec(memory_space=pltpu.SMEM)] + [pl.BlockSpec(memory_space=pltpu.HBM)] * 4,
        out_specs=(pl.BlockSpec(memory_space=pltpu.VMEM),) * 5,
        scratch_shapes=[
            pltpu.VMEM((rows, total), BF16),
            pltpu.VMEM((n, rows, width), BF16),
            pltpu.VMEM((n, AW, width), BF16),
            pltpu.VMEM((n, rows, width), BF16),
            pltpu.VMEM((n, AW, width), BF16),
            pltpu.VMEM((total, width), BF16),
            pltpu.VMEM((rows, width), BF16),
            pltpu.VMEM((width, width), BF16),
            pltpu.VMEM((2, width, width), F32),
            pltpu.VMEM((rows, width), F32),
            pltpu.VMEM((rows, width), F32),
            pltpu.VMEM((width, width), F32),
            pltpu.VMEM((width, width), F32),
            pltpu.VMEM((width, width), F32),
            pltpu.SemaphoreType.DMA((5,)),
            pltpu.SemaphoreType.DMA((4, 2, nz)),
            pltpu.SemaphoreType.DMA((4, nz)),
            pltpu.SemaphoreType.DMA((4, 2 * nz)),
            pltpu.SemaphoreType.DMA((4, n)),
        ],
        compiler_params=pltpu.CompilerParams(
            collective_id=0, has_side_effects=True,
            vmem_limit_bytes=60 * 2 ** 20),
    )(pattern, inverse_rows, lower_panels, link_block, diag_inverse)
    return pl.pallas_call(
        write_out,
        out_shape=shapes,
        in_specs=[pl.BlockSpec(memory_space=pltpu.VMEM)] * 5,
        out_specs=(pl.BlockSpec(memory_space=pltpu.VMEM),) * 5,
    )(*made)


def solution(mesh):
    in_specs = (
        P(("pole", "row"), None),
        P(None, ("pole", "row"), None),
        P("pole", None),
        P(None, "pole", None),
        P(),
    )
    out_specs = (
        P(("pole", "row"), None),
        P(("pole", "row"), None),
        P("pole", None),
        P("pole", None),
        P("pole", None),
    )
    return jax.shard_map(
        functools.partial(shards, mesh.shape["row"]), mesh=mesh,
        in_specs=in_specs, out_specs=out_specs, check_vma=False)
```

time: 170 us -> 49 us (0.29)
  waiting for transfers between devices: 99.1 us -> 0 us
  Pallas kernels: 0 us -> 48.1 us
  blocking collectives: 25.5 us -> 0 us
  between operations: 16.2 us -> 0.64 us
  local copies, waits for them, and re-layouts: 14.5 us -> 0 us
  matrix products: 8.84 us -> 0 us
  other arithmetic: 5.61 us -> 0 us
    psum x1 -> x0, waiting for transfers between devices: 96.8 us -> none  [shards(): diag_total = lax.psum(diag_partial, 'row')]
    pallas_call x0 -> x2, Pallas kernels: none -> 48.1 us  [the longest x1 45.3 us: shards(): pl.pallas_call(functools.partial(kernel, nz), out_shape=shapes, in_specs=...]
    all_gather x1 -> x0, blocking collectives: 25.5 us -> none  [shards(): lax.all_gather(packed_low, 'row', axis=0, tiled=True)]
    gather x4 -> x0, local copies, waits for them, and re-layouts: 10.5 us -> none  [the longest x2 9.39 us: shards(): columns = jnp.take(inverse_rows, picked, axis=1)]
    dot_general x8 -> x0, matrix products: 8.84 us -> none  [the longest x1 2.37 us: shards(): jnp.dot(columns, lax.all_gather(packed_up, 'row', axis=0, tiled=True), pr...]
    all_gather x1 -> x0, waiting for transfers between devices: 2.26 us -> none  [shards(): lax.all_gather(packed_up, 'row', axis=0, tiled=True)]
    sub x2 -> x0, other arithmetic: 2.01 us -> none  [the longest x1 1.22 us: shards(): diag_first = diag_inverse[0] - diag_total]
  transfers between devices with their start and end apart: 2 -> 0, of which waited for: 2 -> 0; matrix products, arithmetic and copies ran while one was open for 8% -> 0% of each run, Pallas kernels for 0% -> 0%
where the time goes in v2:
time: 49 us; the launch traced here: 48.8 us
  Pallas kernels  48.1 us (98%)
  between operations  0.64 us (1%)
    pallas_call x1, Pallas kernels, shards(): pl.pallas_call(functools.partial(kernel, nz), out_shape=shapes, in_specs=...  45.3 us
    pallas_call x1, Pallas kernels, shards(): pl.pallas_call(write_out, out_shape=shapes, in_specs=[pl.BlockSpec(memory...  2.79 us

profile of v2, /device:TPU:0, one launch (start us, length us, event | category | flops | bytes accessed | tf_op | source)
XLA Modules:
  0.0 48.8 jit_solution(14469770134780509386)
XLA Ops:
  0.6 45.3 %shard_map.92 = (bf16[128,384]{1,0:T(8,128)(2,1)}, bf16[128,384]{1,0:T(8,128)(2,1)}, f32[384,384]{1,0:T(8,128)}, f32[384,384]{1,0:T(8,128)}, f32[384,384]{1,0:T(8,128)}) custom-call(s32[2,32]{1,0:T(2,128)} %pat.1, bf16[128,2048]{1,0:T(8,128)(2,1)} %a_hbm.1, bf16[2,128,384]{2,1,0:T(8,128)(2,1)} %lp_hbm.1, bf16[384,384]{1,0:T(8,128)(2,1)} %l_hbm.1, ...), custom_call_target="tpu_custom_call" | custom-call | tf_op jit(solution)/shard_map/pallas_call | solution.py:263
  46.0 2.8 %shard_map.93 = (bf16[128,384]{1,0:T(8,128)(2,1)}, bf16[128,384]{1,0:T(8,128)(2,1)}, f32[384,384]{1,0:T(8,128)}, f32[384,384]{1,0:T(8,128)}, f32[384,384]{1,0:T(8,128)}) custom-call(bf16[128,384]{1,0:T(8,128)(2,1)} %get-tuple-element.10.refs_0_, bf16[128,384]{1,0:T(8,128)(2,1)} %get-tuple-element.11.refs_1_, f32[384,384]{1,0:T(8,128)} %get-tuple-element.12.refs_2_, ...), custom_call_target="tpu_custom_call" | custom-call | tf_op jit(solution)/shard_map/pallas_call | solution.py:293

commit v3 on v2

--- a/solution.py
+++ b/solution.py
@@ -38,8 +38,8 @@
     c = lax.rem(me, 2)
     ox, oc = 1 - x, 1 - c
     width = l_v.shape[1]
-    bufs = (f_v, s_v, p_v, q_v)
-    upper, lower, first, second = range(4)
+    pieces = ((f_v, 0), (f_v, AW), (s_v, 0), (p_v, 0), (p_v, AW), (q_v, 0))
+    upper, lower, first, second = (0, 1), (2,), (3, 4), (5,)
 
     def idx(zz, xx, cc):
         return (zz * 2 + xx) * 2 + cc
@@ -79,8 +79,10 @@
     pl.semaphore_wait(barrier, 2 + (z > 0).astype(jnp.int32) + (z < nz - 1).astype(jnp.int32))
 
     def remote(st, slot, send_sem, target):
+        buf, start = pieces[st]
+        rows = buf.at[slot, pl.ds(start, AW)]
         return pltpu.make_async_remote_copy(
-            src_ref=bufs[st].at[slot], dst_ref=bufs[st].at[slot],
+            src_ref=rows, dst_ref=rows,
             send_sem=send_sem, recv_sem=recv.at[st, slot],
             device_id={"row": target}, device_id_type=MESH)
 
@@ -100,9 +102,9 @@
         for way in (-1, 1):
             @pl.when(inside(z + way))
             def _():
-                zcopy(st, z, way).start()
-        xcopy(st, z).start()
-        ccopy(st, z, x).start()
+                for piece in st:
+                    zcopy(piece, z, way).start()
+        across(st, z)
 
     def at_distance(d, do):
         for way in (-1, 1):
@@ -110,34 +112,38 @@
             def _():
                 do(z + way * d, way)
 
-    def relay(st, zz, way):
-        arrived(st, idx(zz, x, c))
-
-        @pl.when(inside(z - way))
-        def _():
-            zcopy(st, zz, -way).start()
-
     def across(st, zz):
-        xcopy(st, zz).start()
-        ccopy(st, zz, x).start()
+        for piece in st:
+            xcopy(piece, zz).start()
+            ccopy(piece, zz, x).start()
+
+    def relay(st, zz, way, on):
+        for piece in st:
+            arrived(piece, idx(zz, x, c))
+
+            @pl.when(inside(z - way))
+            def _():
+                zcopy(piece, zz, -way).start()
+            if on:
+                across((piece,), zz)
 
     def from_x(st, zz):
-        arrived(st, idx(zz, ox, c))
-        ccopy(st, zz, ox).start()
+        for piece in st:
+            arrived(piece, idx(zz, ox, c))
+            ccopy(piece, zz, ox).start()
 
     def from_core(st, zz, pair):
-        arrived(st, idx(zz, x, oc))
-        pair(zz * 2 + x)
-        arrived(st, idx(zz, ox, oc))
-        pair(zz * 2 + ox)
+        for xx in (x, ox):
+            for piece in st:
+                arrived(piece, idx(zz, xx, oc))
+            pair(zz * 2 + xx)
 
     def gather(one, two, pair_one):
         def z_one(zz, way):
-            relay(one, zz, way)
-            across(one, zz)
+            relay(one, zz, way, True)
 
         def z_two(zz, way):
-            relay(two, zz, way)
+            relay(two, zz, way, False)
 
         at_distance(1, z_one)
         at_distance(1, z_two)
@@ -231,7 +237,7 @@
     d2_out[...] = -accs[...]
 
     def drain(zz, carry):
-        for st in range(4):
+        for st in range(6):
             for way in (-1, 1):
                 sends = zz <= z if way == 1 else zz >= z
 
@@ -281,10 +287,10 @@
             pltpu.VMEM((width, width), F32),
             pltpu.VMEM((width, width), F32),
             pltpu.SemaphoreType.DMA((5,)),
-            pltpu.SemaphoreType.DMA((4, 2, nz)),
-            pltpu.SemaphoreType.DMA((4, nz)),
-            pltpu.SemaphoreType.DMA((4, 2 * nz)),
-            pltpu.SemaphoreType.DMA((4, n)),
+            pltpu.SemaphoreType.DMA((6, 2, nz)),
+            pltpu.SemaphoreType.DMA((6, nz)),
+            pltpu.SemaphoreType.DMA((6, 2 * nz)),
+            pltpu.SemaphoreType.DMA((6, n)),
         ],
         compiler_params=pltpu.CompilerParams(
             collective_id=0, has_side_effects=True,

time: 49 us -> 47.9 us (0.978)
  Pallas kernels: 48.1 us -> 47.1 us
    pallas_call x1, Pallas kernels: 45.3 us -> 44.3 us  [shards(): pl.pallas_call(functools.partial(kernel, nz), out_shape=shapes, in_specs=...]
where the time goes in v3:
time: 47.9 us; the launch traced here: 47.8 us
  Pallas kernels  47.1 us (98%)
  between operations  0.64 us (1%)
    pallas_call x1, Pallas kernels, shards(): pl.pallas_call(functools.partial(kernel, nz), out_shape=shapes, in_specs=...  44.3 us
    pallas_call x1, Pallas kernels, shards(): pl.pallas_call(write_out, out_shape=shapes, in_specs=[pl.BlockSpec(memory...  2.79 us

profile of v3, /device:TPU:0, one launch (start us, length us, event | category | flops | bytes accessed | tf_op | source)
XLA Modules:
  0.0 47.8 jit_solution(5643204525679157072)
XLA Ops:
  0.6 44.3 %shard_map.92 = (bf16[128,384]{1,0:T(8,128)(2,1)}, bf16[128,384]{1,0:T(8,128)(2,1)}, f32[384,384]{1,0:T(8,128)}, f32[384,384]{1,0:T(8,128)}, f32[384,384]{1,0:T(8,128)}) custom-call(s32[2,32]{1,0:T(2,128)} %pat.1, bf16[128,2048]{1,0:T(8,128)(2,1)} %a_hbm.1, bf16[2,128,384]{2,1,0:T(8,128)(2,1)} %lp_hbm.1, bf16[384,384]{1,0:T(8,128)(2,1)} %l_hbm.1, ...), custom_call_target="tpu_custom_call" | custom-call | tf_op jit(solution)/shard_map/pallas_call | solution.py:269
  45.0 2.8 %shard_map.93 = (bf16[128,384]{1,0:T(8,128)(2,1)}, bf16[128,384]{1,0:T(8,128)(2,1)}, f32[384,384]{1,0:T(8,128)}, f32[384,384]{1,0:T(8,128)}, f32[384,384]{1,0:T(8,128)}) custom-call(bf16[128,384]{1,0:T(8,128)(2,1)} %get-tuple-element.10.refs_0_, bf16[128,384]{1,0:T(8,128)(2,1)} %get-tuple-element.11.refs_1_, f32[384,384]{1,0:T(8,128)} %get-tuple-element.12.refs_2_, ...), custom_call_target="tpu_custom_call" | custom-call | tf_op jit(solution)/shard_map/pallas_call | solution.py:299

commit v4 on v3

--- a/solution.py
+++ b/solution.py
@@ -138,14 +138,15 @@
                 arrived(piece, idx(zz, xx, oc))
             pair(zz * 2 + xx)
 
-    def gather(one, two, pair_one):
+    def gather(one, two, pair_one, begun):
         def z_one(zz, way):
             relay(one, zz, way, True)
 
         def z_two(zz, way):
             relay(two, zz, way, False)
 
-        at_distance(1, z_one)
+        if not begun:
+            at_distance(1, z_one)
         at_distance(1, z_two)
         from_x(one, z)
         from_core(one, z, pair_one)
@@ -160,7 +161,7 @@
 
         lax.fori_loop(2, nz + 1, step, 0)
 
-    def finish(two, pair_two):
+    def finish(two, pair_two, following):
         from_x(two, z)
 
         def turn(d, carry):
@@ -168,6 +169,8 @@
             return carry
 
         lax.fori_loop(1, nz, turn, 0)
+        if following:
+            at_distance(1, lambda zz, way: relay(following, zz, way, True))
         from_core(two, z, pair_two)
 
         def turn_core(d, carry):
@@ -208,7 +211,7 @@
     cp_l.wait()
     cp_d.wait()
 
-    gather(upper, lower, pair_upper)
+    gather(upper, lower, pair_upper, False)
     for i, mark in enumerate((up0, up1)):
         rows = pl.ds(i * AW, AW)
         p_v[me, rows, :] = keep(mark, -acc1[rows, :]).astype(BF16)
@@ -217,14 +220,14 @@
     p1 = p_v[me]
     p1_out[...] = p1
     acc2[...] += dot(p1, l_v[...])
-    finish(lower, pair_lower)
+    finish(lower, pair_lower, first)
     far = (-acc2[...]).astype(BF16)
     q_v[me] = jnp.where(low0 != 0, far[:AW], far[AW:])
     send_own(second)
     p2_out[pl.ds(0, AW), :] = keep(low0, far[:AW])
     p2_out[pl.ds(AW, AW), :] = keep(low1, far[AW:])
 
-    gather(first, second, pair_first)
+    gather(first, second, pair_first, True)
     link = l_v[...]
     diag = d_v[0] - accd[...]
     d1_out[...] = diag
@@ -233,7 +236,7 @@
     c_out[...] = cross
     hi, lo = split2(cross)
     accs[...] = (dot_t(link, hi) + dot_t(link, lo)) - d_v[1]
-    finish(second, pair_second)
+    finish(second, pair_second, ())
     d2_out[...] = -accs[...]
 
     def drain(zz, carry):

time: 47.9 us -> 50.8 us (1.061)
  Pallas kernels: 47.1 us -> 50 us
    pallas_call x1, Pallas kernels: 44.3 us -> 47.2 us  [shards(): pl.pallas_call(functools.partial(kernel, nz), out_shape=shapes, in_specs=...]
where the time goes in v4:
time: 50.8 us; the launch traced here: 50.6 us
  Pallas kernels  50 us (98%)
  between operations  0.64 us (1%)
    pallas_call x1, Pallas kernels, shards(): pl.pallas_call(functools.partial(kernel, nz), out_shape=shapes, in_specs=...  47.2 us
    pallas_call x1, Pallas kernels, shards(): pl.pallas_call(write_out, out_shape=shapes, in_specs=[pl.BlockSpec(memory...  2.79 us

profile of v4, /device:TPU:0, one launch (start us, length us, event | category | flops | bytes accessed | tf_op | source)
XLA Modules:
  0.0 50.6 jit_solution(12979385392186860040)
XLA Ops:
  0.6 47.2 %shard_map.92 = (bf16[128,384]{1,0:T(8,128)(2,1)}, bf16[128,384]{1,0:T(8,128)(2,1)}, f32[384,384]{1,0:T(8,128)}, f32[384,384]{1,0:T(8,128)}, f32[384,384]{1,0:T(8,128)}) custom-call(s32[2,32]{1,0:T(2,128)} %pat.1, bf16[128,2048]{1,0:T(8,128)(2,1)} %a_hbm.1, bf16[2,128,384]{2,1,0:T(8,128)(2,1)} %lp_hbm.1, bf16[384,384]{1,0:T(8,128)(2,1)} %l_hbm.1, ...), custom_call_target="tpu_custom_call" | custom-call | tf_op jit(solution)/shard_map/pallas_call | solution.py:272
  47.9 2.8 %shard_map.93 = (bf16[128,384]{1,0:T(8,128)(2,1)}, bf16[128,384]{1,0:T(8,128)(2,1)}, f32[384,384]{1,0:T(8,128)}, f32[384,384]{1,0:T(8,128)}, f32[384,384]{1,0:T(8,128)}) custom-call(bf16[128,384]{1,0:T(8,128)(2,1)} %get-tuple-element.10.refs_0_, bf16[128,384]{1,0:T(8,128)(2,1)} %get-tuple-element.11.refs_1_, f32[384,384]{1,0:T(8,128)} %get-tuple-element.12.refs_2_, ...), custom_call_target="tpu_custom_call" | custom-call | tf_op jit(solution)/shard_map/pallas_call | solution.py:302
